TPU v7x, 256 devices: a whole 4x4x8 slice. The times are simulated.
256 devices in a mesh: req: 8 (over y, core), kv: 32 (over z, x).
Axes of the slice: x: 4, y: 4, z: 8, core: 2. Of those that a mesh axis runs over, the one named last changes fastest.
Arguments:
- q_nope: bfloat16 [32, 128, 128], P('req', 'kv'), may hold values from -6 to 6
- q_rope: bfloat16 [32, 128, 64], P('req', 'kv'), may hold values from -8 to 8
- cache: bfloat16 [32, 65536, 576], P('req', 'kv'), may hold values from -14 to 14
- lengths: int32 [32], P('req'), may hold values from 2 to 65536, as said below
- w_uk: bfloat16 [128, 128, 512], P('kv'), may hold values from -0.5 to 0.5
- w_uv: bfloat16 [128, 512, 128], P('kv'), may hold values from -0.25 to 0.25
Outputs:
- attn: bfloat16 [32, 16384], P('req', 'kv')
Inputs may be any that keep to these rules, and one draw needn't show every extreme that they name: `lengths`: some request has exactly 65536.
All inputs are finite; a program needn't handle non-finite values.
Results may differ from a plain program's by a relative error of at most 0.0084.
Values may be sent and summed in bfloat16 or wider, within the bound.
A program may use at most 128 MiB of HBM per device.

v0:
```python
import jax
import jax.numpy as jnp
from jax import lax
from jax.sharding import PartitionSpec as P


def local(q_nope, q_rope, cache, lengths, w_uk, w_uv):
    heads_dev = q_nope.shape[1]
    latent_width = w_uk.shape[2]
    split_len = cache.shape[1]
    score_scale = (q_nope.shape[2] + q_rope.shape[2]) ** (-0.5)
    q_lat = jnp.einsum("bhd,hdc->bhc", q_nope, w_uk, preferred_element_type=jnp.float32).astype(
        jnp.bfloat16
    )
    query_full = jnp.concatenate([q_lat, q_rope], axis=2)
    queries_all = lax.all_gather(query_full, "kv", axis=1, tiled=True)
    scores = (
        jnp.einsum("bhk,btk->bht", queries_all, cache, preferred_element_type=jnp.float32)
        * score_scale
    )
    positions = lax.axis_index("kv") * split_len + jnp.arange(split_len, dtype=jnp.int32)
    is_live = positions[None, None, :] < lengths[:, None, None]
    scores = jnp.where(is_live, scores, jnp.float32(-1e30))
    top_local = jnp.max(scores, axis=2)
    weights = jnp.where(is_live, jnp.exp(scores - top_local[:, :, None]), jnp.float32(0.0))
    local_sum = jnp.sum(weights, axis=2)
    local_out = jnp.einsum(
        "bht,btc->bhc",
        weights.astype(jnp.bfloat16),
        cache[:, :, :latent_width],
        preferred_element_type=jnp.float32,
    )
    head_start = lax.axis_index("kv") * heads_dev
    top_score = lax.pmax(top_local, "kv")
    factor = jnp.exp(top_local - top_score)
    summed_out, summed_den = lax.psum((local_out * factor[:, :, None], local_sum * factor), "kv")
    numerator = lax.dynamic_slice_in_dim(summed_out, head_start, heads_dev, 1)
    denominator = lax.dynamic_slice_in_dim(summed_den, head_start, heads_dev, 1)
    latent_out = (numerator / denominator[:, :, None]).astype(jnp.bfloat16)
    attn = jnp.einsum("bhc,hcv->bhv", latent_out, w_uv, preferred_element_type=jnp.float32).astype(
        jnp.bfloat16
    )
    return attn.reshape(attn.shape[0], heads_dev * attn.shape[2])


def solution(mesh):
    in_specs = (
        P("req", "kv", None),
        P("req", "kv", None),
        P("req", "kv", None),
        P("req"),
        P("kv", None, None),
        P("kv", None, None),
    )
    out_specs = P("req", "kv")
    return jax.shard_map(local, mesh=mesh, in_specs=in_specs, out_specs=out_specs, check_vma=False)
```

profile of v0, /device:TPU:8, one launch (start us, length us, event | category | flops | bytes accessed | tf_op | source)
XLA Modules:
  0.0 302.3 jit_solution(17117205833248305423)
XLA Ops:
  6.5 0.0 copy-start
  6.5 0.0 all-reduce.2.cloned.1.call-start
  6.5 0.7 copy.9
  7.3 0.3 copy-done
  7.6 0.9 fusion.11
  8.5 52.9 %all_gather.3 = bf16[4,128,576]{2,0,1:T(4,128)(2,1)S(1)} all-gather(bf16[4,4,576]{2,0,1:T(4,128)(2,1)S(1)} %pad_maximum_fusion), channel_id=1, replica_groups=mesh['req'=8,'kv'=32] {'kv'}, dimensions={1}, use_global_device_ids=true | all-gather | bytes 608256 | tf_op jit(solution)/shard_map/all_gather | solution.py:16
  61.4 0.0 slice-start
  61.4 0.9 broadcast_compare_fusion
  62.3 0.0 slice-start.1
  62.3 0.0 slice-start.2
  62.3 6.3 %fusion.2 = (f32[4,128]{1,0:T(4,128)S(1)}, f32[4,128,2048]{2,1,0:T(8,128)S(1)}) fusion(pred[4,2048]{1,0:T(4,128)(4,1)S(1)} %broadcast_compare_fusion, bf16[4,2048,576]{1,2,0:T(8,128)(2,1)} %param.8, bf16[4,128,576]{2,0,1:T(4,128)(2,1)S(1)} %all_gather.3), kind=kOutput, calls=%fused_computation.4 | convolution fusion | flops 1211104768 | bytes 14231552 | tf_op jit(solution)/shard_map/bhk,btk->bht/dot_general | solution.py:18
  68.7 1.2 fusion.3
  69.9 0.0 slice-done
  69.9 0.0 slice-done.1
  69.9 0.0 slice-done.2
  69.9 0.0 copy-start.1
  69.9 3.5 %fusion = f32[4,128,512]{2,1,0:T(8,128)S(1)} fusion(bf16[4,2048,576]{1,2,0:T(8,128)(2,1)S(1)} %bitcast.10, f32[4,128,2048]{2,1,0:T(8,128)S(1)} %get-tuple-element.8, f32[4,128]{1,0:T(4,128)S(1)} %get-tuple-element.7, pred[4,2048]{1,0:T(4,128)(4,1)S(1)} %broadcast_compare_fusion), kind=kOutput, calls=%fused_computation | convolution fusion | flops 1078984704 | bytes 13641728 | tf_op jit(solution)/shard_map/bht,btc->bhc/dot_general | solution.py:27
  73.4 72.3 %pmax.7 = f32[4,128]{1,0:T(4,128)S(1)} all-reduce(f32[4,128]{1,0:T(4,128)S(1)} %get-tuple-element.7), channel_id=1, replica_groups=mesh['req'=8,'kv'=32] {'kv'}, use_global_device_ids=true, to_apply=%region_1.2 | all-reduce | flops 512 | bytes 4096 | tf_op jit(solution)/shard_map/pmax | solution.py:34
  145.7 0.1 copy.11
  145.8 1.8 copy_multiply_fusion
  147.6 0.0 all-reduce.2.cloned.1.call-update
  147.6 69.7 %psum.15 = f32[4,128]{1,0:T(4,128)S(1)} all-reduce(f32[4,128]{1,0:T(4,128)S(1)} %get-tuple-element.5), channel_id=1, replica_groups=mesh['req'=8,'kv'=32] {'kv'}, use_global_device_ids=true, to_apply=%region_4.5 | all-reduce | flops 512 | bytes 4096 | tf_op jit(solution)/shard_map/psum | solution.py:36
  217.3 0.1 constant_dynamic-slice_fusion
  217.4 0.1 copy.12
  217.5 76.3 %all-reduce.2.cloned.1.call-done = f32[4,128,512]{2,0,1:T(4,128)} async-done(((f32[4,128,512]{2,0,1:T(4,128)}), f32[4,128,512]{2,0,1:T(4,128)}) %all-reduce.2.cloned.1.call-update) | async-done | bytes 1048592 | tf_op jit(solution)/shard_map/psum | solution.py:36
  293.8 0.0 copy-done.1
  293.8 1.6 fusion.12
  (4 shorter events, 0.0 us)
Async XLA Ops:
  6.5 1.1 copy-start
  6.5 287.3 %all-reduce.2.cloned.1.call-start = ((), (), s32[]{:S(2)}) async-start(), calls=%async_computation | async-start | bytes 2097152 | tf_op jit(solution)/shard_map/psum | solution.py:36
  61.4 8.5 %slice-start = ((s8[9437184]{0:T(1024)(128)(4,1)}), s8[4194304]{0:T(1024)(128)(4,1)S(1)}, s32[]{:S(2)}) async-start(s8[9437184]{0:T(1024)(128)(4,1)} %bitcast.9), calls=%async_computation.1 | async-start | bytes 8388608
  62.3 7.6 %slice-start.1 = ((s8[9437184]{0:T(1024)(128)(4,1)}), s8[4194304]{0:T(1024)(128)(4,1)S(1)}, s32[]{:S(2)}) async-start(s8[9437184]{0:T(1024)(128)(4,1)} %bitcast.9), calls=%async_computation.2 | async-start | bytes 8388608
  62.3 7.6 %slice-start.2 = ((s8[9437184]{0:T(1024)(128)(4,1)}), s8[1048576]{0:T(1024)(128)(4,1)S(1)}, s32[]{:S(2)}) async-start(s8[9437184]{0:T(1024)(128)(4,1)} %bitcast.9), calls=%async_computation.3 | async-start | bytes 2097152
  69.9 223.9 %copy-start.1 = (bf16[4,512,128]{2,1,0:T(8,128)(2,1)S(1)}, bf16[4,512,128]{2,1,0:T(8,128)(2,1)}, u32[]{:S(2)}) copy-start(bf16[4,512,128]{2,1,0:T(8,128)(2,1)} %param.11) | copy-start | bytes 1572868
Sparse Core Ops, SparseCore 0:
  147.7 146.0 all-reduce.1
where the time goes:
time: 302 us
  blocking collectives  195 us (65%)
  waiting for transfers between devices  76.4 us (25%)
  between operations  13.5 us (4%)
  matrix products  12.2 us (4%)
  other arithmetic  3.94 us (1%)
    psum x1, waiting for transfers between devices, local(): lax.psum((local_out * factor[:, :, None], local_sum * factor), 'kv')  76.3 us
    pmax x1, blocking collectives, local(): top_score = lax.pmax(top_local, 'kv')  72.3 us
    psum x1, blocking collectives, local(): lax.psum((local_out * factor[:, :, None], local_sum * factor), 'kv')  69.7 us
    all_gather x1, blocking collectives, local(): queries_all = lax.all_gather(query_full, 'kv', axis=1, tiled=True)  52.9 us
    dot_general x1, matrix products, local(): jnp.einsum('bhk,btk->bht', queries_all, cache, preferred_element_type=jnp...  6.31 us
  transfers between devices with their start and end apart: 1, of which 1 were waited for; matrix products, arithmetic and copies ran while one was open for 0% of the time, Pallas kernels for 0%

commit v1 on v0

v1 whole, which is shorter than its diff:
```python
import functools
import math

import jax
import jax.numpy as jnp
from jax import lax
from jax.experimental import pallas as pl
from jax.experimental.pallas import tpu as pltpu
from jax.sharding import PartitionSpec as P

MESH = pl.DeviceIdType.MESH
F32 = jnp.float32
BF16 = jnp.bfloat16
NX, NZ = 4, 8
NB, NH = 4, 4
LANES = 128
DEAD = -1e30
CHUNK = 512


def stats_tile(top, total):
    lane = lax.broadcasted_iota(jnp.int32, (top.shape[0], LANES), 1)
    top_hi = top.astype(BF16).astype(F32)
    sum_hi = total.astype(BF16).astype(F32)
    first = jnp.where(lane < 32, top_hi, top - top_hi)
    second = jnp.where(lane < 96, sum_hi, total - sum_hi)
    return jnp.where(lane < 64, first, second)


def read_stats(tile):
    return tile[:, 0:1] + tile[:, 32:33], tile[:, 64:65] + tile[:, 96:97]


def kernel(
    scale,
    lengths,
    q_nope,
    q_rope,
    w_uk_hbm,
    w_uv_hbm,
    cache_hbm,
    out,
    w_uk,
    w_uv,
    cache,
    gathered,
    flat,
    rope_flat,
    query,
    scores,
    probs,
    x_send,
    x_recv,
    turn,
    z_send,
    z_recv,
    latent,
    local_sem,
    gz_send_sem,
    gz_recv_sem,
    gx_send_sem,
    gx_recv_sem,
    rx_send_sem,
    rx_recv_sem,
    rz_send_sem,
    rz_recv_sem,
):
    req = lax.axis_index("req")
    kv = lax.axis_index("kv")
    z = lax.div(kv, NX)
    x = lax.rem(kv, NX)
    split_len = cache.shape[2]
    latent_width = w_uk.shape[2]
    z_order = (4, 3, 5, 2, 6, 1, 7)
    x_order = (2, 1, 3)

    def z_at(d):
        return lax.rem(z + d, NZ)

    def x_at(d):
        return lax.rem(x + d, NX)

    barrier = pltpu.get_barrier_semaphore()
    for d in z_order:
        pl.semaphore_signal(barrier, inc=1, device_id=(req, z_at(d) * NX + x), device_id_type=MESH)
    for d in x_order:
        pl.semaphore_signal(barrier, inc=1, device_id=(req, z * NX + x_at(d)), device_id_type=MESH)

    uk_copy = pltpu.make_async_copy(w_uk_hbm, w_uk, local_sem.at[4])
    uk_copy.start()

    def cache_copy(b):
        return pltpu.make_async_copy(cache_hbm.at[b], cache.at[b], local_sem.at[b])

    for b in range(NB):
        cache_copy(b).start()
    uv_copy = pltpu.make_async_copy(w_uv_hbm, w_uv, local_sem.at[5])
    uv_copy.start()

    def gz_copy(b, source, d):
        return pltpu.make_async_remote_copy(
            src_ref=gathered.at[b, x, source],
            dst_ref=gathered.at[b, x, source],
            send_sem=gz_send_sem.at[b, d],
            recv_sem=gz_recv_sem.at[b, source],
            device_id=(req, z_at(d) * NX + x),
            device_id_type=MESH,
        )

    def gx_copy(b, source, d):
        return pltpu.make_async_remote_copy(
            src_ref=gathered.at[b, source],
            dst_ref=gathered.at[b, source],
            send_sem=gx_send_sem.at[b, d],
            recv_sem=gx_recv_sem.at[b, source],
            device_id=(req, z * NX + x_at(d)),
            device_id_type=MESH,
        )

    def rx_copy(b, source, d):
        return pltpu.make_async_remote_copy(
            src_ref=x_send.at[b, pl.ds(pl.multiple_of(x_at(d) * 32, 32), 32)],
            dst_ref=x_recv.at[b, source],
            send_sem=rx_send_sem.at[b, d],
            recv_sem=rx_recv_sem.at[b, source],
            device_id=(req, z * NX + x_at(d)),
            device_id_type=MESH,
        )

    def rz_copy(b, source, d):
        return pltpu.make_async_remote_copy(
            src_ref=z_send.at[b, z_at(d)],
            dst_ref=z_recv.at[b, source],
            send_sem=rz_send_sem.at[b, d],
            recv_sem=rz_recv_sem.at[b, source],
            device_id=(req, z_at(d) * NX + x),
            device_id_type=MESH,
        )

    rope_flat[0:16, :] = jnp.zeros((16, LANES), F32)
    for b in range(NB):
        flat[b * NH : (b + 1) * NH, :] = q_nope[b].astype(F32)
        rope_flat[b * NH : (b + 1) * NH, 0:64] = q_rope[b].astype(F32)
    gathered[NB, x, z] = rope_flat[0:16, :].astype(BF16)
    rows = flat[0:16, :]
    head = lax.rem(lax.broadcasted_iota(jnp.int32, (16, LANES), 0), NH)
    uk_copy.wait()
    q_lat = jnp.zeros((16, latent_width), F32)
    for h in range(NH):
        own = jnp.where(head == h, rows, 0.0).astype(BF16)
        q_lat = q_lat + jnp.dot(own, w_uk[h], preferred_element_type=F32)
    for b in range(NB):
        for j in range(4):
            flat[b * 16 + j * NH : b * 16 + (j + 1) * NH, :] = q_lat[
                b * NH : (b + 1) * NH, j * LANES : (j + 1) * LANES
            ]
    for b in range(NB):
        gathered[b, x, z] = flat[b * 16 : (b + 1) * 16, :].astype(BF16)

    pl.semaphore_wait(barrier, NZ - 1 + NX - 1)

    for b in (NB, 0, 1, 2, 3):
        for d in z_order:
            gz_copy(b, z, d).start()
    for b in (NB, 0, 1, 2, 3):
        for d in z_order:
            gz_copy(b, z_at(d), d).wait_recv()
        for d in x_order:
            gx_copy(b, x, d).start()

    for d in x_order:
        gx_copy(NB, x_at(d), d).wait_recv()
    rope_flat[...] = gathered[NB].reshape(NX * NZ * 16, LANES).astype(F32)

    position = kv * split_len + lax.broadcasted_iota(jnp.int32, (1, CHUNK), 1)

    def attend(b, carry):
        for d in x_order:
            gx_copy(b, x_at(d), d).wait_recv()
        flat[...] = gathered[b].reshape(NX * NZ * 16, LANES).astype(F32)
        for xs in range(NX):
            for hp in range(0, NH, 2):
                at = xs * 32 + hp * 8
                for j in range(4):
                    pair = [
                        flat[pl.ds(xs * 128 + j * NH + h, 8, stride=16), :] for h in (hp, hp + 1)
                    ]
                    query[at : at + 16, j * LANES : (j + 1) * LANES] = jnp.concatenate(
                        pair, axis=0
                    ).astype(BF16)
                pair = [
                    rope_flat[pl.ds(xs * 128 + b * NH + h, 8, stride=16), :] for h in (hp, hp + 1)
                ]
                query[at : at + 16, 512:640] = jnp.concatenate(pair, axis=0).astype(BF16)
        cache_copy(b).wait()
        q = query[:, 0:576]
        length = lengths[b]
        peak = None
        for c in range(0, split_len, CHUNK):
            s = jnp.dot(q, cache[b, :, c : c + CHUNK], preferred_element_type=F32)
            s = jnp.where(position + c < length, s, DEAD)
            scores[:, c : c + CHUNK] = s
            for k in range(0, CHUNK, LANES):
                piece = s[:, k : k + LANES]
                peak = piece if peak is None else jnp.maximum(peak, piece)
        top = jnp.max(peak, axis=1, keepdims=True) * scale
        top_hi = top.astype(BF16).astype(F32)
        top = top_hi + (top - top_hi).astype(BF16).astype(F32)
        total = jnp.zeros((128, LANES), F32)
        for c in range(0, split_len, CHUNK):
            p = jnp.exp2(scores[:, c : c + CHUNK] * scale - top)
            probs[:, c : c + CHUNK] = p.astype(BF16)
            for k in range(0, CHUNK, LANES):
                total = total + p[:, k : k + LANES]
        o = lax.dot_general(
            probs[...], cache[b, 0:512, :], (((1,), (1,)), ((), ())), preferred_element_type=F32
        )
        x_send[b, :, 0:512] = o.astype(BF16)
        x_send[b, :, 512:640] = stats_tile(top, jnp.sum(total, axis=1, keepdims=True)).astype(BF16)
        for d in x_order:
            rx_copy(b, x, d).start()
        return carry

    lax.fori_loop(0, NB, attend, 0)

    def reduce_x(b, carry):
        for d in x_order:
            rx_copy(b, x_at(d), d).wait_recv()
        parts = [x_send[b, pl.ds(pl.multiple_of(x * 32, 32), 32), :].astype(F32)]
        for d in x_order:
            parts.append(x_recv[b, x_at(d)].astype(F32))
        stats = [read_stats(part[:, 512:640]) for part in parts]
        top = functools.reduce(jnp.maximum, [t for t, _ in stats])
        acc, total = None, None
        for part, (t, s) in zip(parts, stats):
            w = jnp.exp2(t - top)
            acc = part[:, 0:512] * w if acc is None else acc + part[:, 0:512] * w
            total = s * w if total is None else total + s * w
        info = stats_tile(top, total)
        for h in range(NH):
            for j in range(4):
                r = h * 4 + j
                turn[r * 8 : r * 8 + 8, :] = acc[h * 8 : h * 8 + 8, j * LANES : (j + 1) * LANES]
                turn[128 + r * 8 : 128 + r * 8 + 8, :] = info[h * 8 : h * 8 + 8, :]
        for zs in range(NZ):
            z_send[b, zs] = turn[pl.ds(zs, 32, stride=8), :].astype(BF16)
        for d in z_order:
            rz_copy(b, z, d).start()
        return carry

    lax.fori_loop(0, NB, reduce_x, 0)

    def reduce_z(b, carry):
        for d in z_order:
            rz_copy(b, z_at(d), d).wait_recv()
        parts = [z_send[b, z].astype(F32)] + [z_recv[b, z_at(d)].astype(F32) for d in z_order]
        stats = [read_stats(part[16:32]) for part in parts]
        top = functools.reduce(jnp.maximum, [t for t, _ in stats])
        acc, total = None, None
        for part, (t, s) in zip(parts, stats):
            w = jnp.exp2(t - top)
            acc = part[0:16] * w if acc is None else acc + part[0:16] * w
            total = s * w if total is None else total + s * w
        latent[pl.ds(pl.multiple_of(b * 16, 16), 16), :] = acc / total
        return carry

    lax.fori_loop(0, NB, reduce_z, 0)

    uv_copy.wait()
    for h in range(NH):
        lat = jnp.concatenate(
            [latent[pl.ds(h * 4 + j, NB, stride=16), :] for j in range(4)], axis=1
        ).astype(BF16)
        out[:, h * LANES : (h + 1) * LANES] = jnp.dot(
            lat, w_uv[h], preferred_element_type=F32
        ).astype(BF16)

    def drain(b, carry):
        for d in z_order:
            gz_copy(b, z, d).wait_send()
            rz_copy(b, z, d).wait_send()
        for d in x_order:
            gx_copy(b, x, d).wait_send()
            rx_copy(b, x, d).wait_send()
        return carry

    lax.fori_loop(0, NB, drain, 0)
    for d in z_order:
        gz_copy(NB, z, d).wait_send()
    for d in x_order:
        gx_copy(NB, x, d).wait_send()


def local(q_nope, q_rope, cache, lengths, w_uk, w_uv):
    scale = (q_nope.shape[2] + q_rope.shape[2]) ** (-0.5) * math.log2(math.e)
    cache_t = jnp.swapaxes(cache, 1, 2)
    vmem = pl.BlockSpec(memory_space=pltpu.VMEM)
    hbm = pl.BlockSpec(memory_space=pl.ANY)
    dma = pltpu.SemaphoreType.DMA
    return pl.pallas_call(
        functools.partial(kernel, scale),
        out_shape=jax.ShapeDtypeStruct((NB, NH * w_uv.shape[2]), BF16),
        in_specs=[pl.BlockSpec(memory_space=pltpu.SMEM), vmem, vmem, hbm, hbm, hbm],
        out_specs=vmem,
        scratch_shapes=[
            pltpu.VMEM(w_uk.shape, BF16),
            pltpu.VMEM(w_uv.shape, BF16),
            pltpu.VMEM(cache_t.shape, BF16),
            pltpu.VMEM((NB + 1, NX, NZ, 16, LANES), BF16),
            pltpu.VMEM((NX * NZ * 16, LANES), F32),
            pltpu.VMEM((NX * NZ * 16, LANES), F32),
            pltpu.VMEM((128, 640), BF16),
            pltpu.VMEM((128, cache_t.shape[2]), F32),
            pltpu.VMEM((128, cache_t.shape[2]), BF16),
            pltpu.VMEM((NB, 128, 640), BF16),
            pltpu.VMEM((NB, NX, 32, 640), BF16),
            pltpu.VMEM((256, LANES), F32),
            pltpu.VMEM((NB, NZ, 32, LANES), BF16),
            pltpu.VMEM((NB, NZ, 32, LANES), BF16),
            pltpu.VMEM((NB * 16, LANES), F32),
            dma((6,)),
            dma((NB + 1, NZ)),
            dma((NB + 1, NZ)),
            dma((NB + 1, NX)),
            dma((NB + 1, NX)),
            dma((NB, NX)),
            dma((NB, NX)),
            dma((NB, NZ)),
            dma((NB, NZ)),
        ],
        compiler_params=pltpu.CompilerParams(
            collective_id=0, has_side_effects=True, vmem_limit_bytes=48 * 2**20
        ),
    )(lengths, q_nope, q_rope, w_uk, w_uv, cache_t)


def solution(mesh):
    in_specs = (
        P("req", "kv", None),
        P("req", "kv", None),
        P("req", "kv", None),
        P("req"),
        P("kv", None, None),
        P("kv", None, None),
    )
    return jax.shard_map(
        local, mesh=mesh, in_specs=in_specs, out_specs=P("req", "kv"), check_vma=False
    )
```

time: 302 us -> 41.8 us (0.14)
  blocking collectives: 195 us -> 0 us
  waiting for transfers between devices: 76.4 us -> 0 us
  Pallas kernels: 0 us -> 36.9 us
  between operations: 13.5 us -> 0.01 us
  matrix products: 12.2 us -> 0 us
  other arithmetic: 3.94 us -> 0 us
  local copies, waits for them, and re-layouts: 1.36 us -> 4.7 us
    psum x1 -> x0, waiting for transfers between devices: 76.3 us -> none  [local(): lax.psum((local_out * factor[:, :, None], local_sum * factor), 'kv')]
    pmax x1 -> x0, blocking collectives: 72.3 us -> none  [local(): top_score = lax.pmax(top_local, 'kv')]
    psum x1 -> x0, blocking collectives: 69.7 us -> none  [local(): lax.psum((local_out * factor[:, :, None], local_sum * factor), 'kv')]
    all_gather x1 -> x0, blocking collectives: 52.9 us -> none  [local(): queries_all = lax.all_gather(query_full, 'kv', axis=1, tiled=True)]
    pallas_call x0 -> x1, Pallas kernels: none -> 36.9 us  [local(): pl.pallas_call(functools.partial(kernel, scale), out_shape=jax.ShapeDtype...]
    dot_general x4 -> x0, matrix products: 12.2 us -> none  [the longest x1 6.31 us: local(): jnp.einsum('bhk,btk->bht', queries_all, cache, preferred_element_type=jnp...]
    unnamed x11, local copies, waits for them, and re-layouts: 1.07 us -> 4.7 us
  transfers between devices with their start and end apart: 1 -> 0, of which waited for: 1 -> 0; matrix products, arithmetic and copies ran while one was open for 0% -> 0% of each run, Pallas kernels for 0% -> 0%
where the time goes in v1:
time: 41.8 us; the launch traced here: 41.6 us
  Pallas kernels  36.9 us (88%)
  local copies, waits for them, and re-layouts  4.7 us (11%)
    pallas_call x1, Pallas kernels, local(): pl.pallas_call(functools.partial(kernel, scale), out_shape=jax.ShapeDtype...  36.9 us
    unnamed x11, local copies, waits for them, and re-layouts  4.7 us

profile of v1, /device:TPU:8, one launch (start us, length us, event | category | flops | bytes accessed | tf_op | source)
XLA Modules:
  0.0 41.6 jit_solution(1881124341457060678)
XLA Ops:
  0.0 0.0 copy-start
  0.0 1.0 %copy-done = bf16[4,128,512]{2,1,0:T(8,128)(2,1)S(1)} copy-done((bf16[4,128,512]{2,1,0:T(8,128)(2,1)S(1)}, bf16[4,128,512]{2,1,0:T(8,128)(2,1)}, u32[]{:S(2)}) %copy-start) | copy-done | bytes 524312
  1.0 0.0 copy-start.1
  1.0 1.0 %copy-done.1 = bf16[4,512,128]{2,1,0:T(8,128)(2,1)S(1)} copy-done((bf16[4,512,128]{2,1,0:T(8,128)(2,1)S(1)}, bf16[4,512,128]{2,1,0:T(8,128)(2,1)}, u32[]{:S(2)}) %copy-start.1) | copy-done | bytes 524312
  2.1 0.0 copy-start.2
  2.1 0.7 %copy-done.2 = bf16[4,4,128]{2,1,0:T(4,128)(2,1)S(1)} copy-done((bf16[4,4,128]{2,1,0:T(4,128)(2,1)S(1)}, bf16[4,4,128]{2,1,0:T(4,128)(2,1)}, u32[]{:S(2)}) %copy-start.2) | copy-done | bytes 4120
  2.8 0.0 copy-start.3
  2.8 0.7 %copy-done.3 = bf16[4,4,64]{2,1,0:T(4,128)(2,1)S(1)} copy-done((bf16[4,4,64]{2,1,0:T(4,128)(2,1)S(1)}, bf16[4,4,64]{2,1,0:T(4,128)(2,1)}, u32[]{:S(2)}) %copy-start.3) | copy-done | bytes 2072
  3.5 0.0 copy-start.4
  3.5 0.7 %copy-done.4 = s32[4]{0:T(128)S(1)} copy-done((s32[4]{0:T(128)S(1)}, s32[4]{0:T(128)}, u32[]{:S(2)}) %copy-start.4) | copy-done | bytes 40
  4.1 36.9 %shard_map.64 = bf16[4,512]{1,0:T(4,128)(2,1)S(1)} custom-call(s32[4]{0:T(128)S(1)} %copy-done.4, bf16[4,4,128]{2,1,0:T(4,128)(2,1)S(1)} %copy-done.2, bf16[4,4,64]{2,1,0:T(4,128)(2,1)S(1)} %copy-done.3, bf16[4,128,512]{2,1,0:T(8,128)(2,1)S(1)} %copy-done, bf16[4,512,128]{2,1,0:T(8,128)(2,1)S(1)} %copy-done.1, bf16[4,576,2048]{2,1,0:T(8,128)(2,1)} %bitcast.1), custom_call_target="tpu_custom_call" | custom-call | tf_op jit(solution)/shard_map/pallas_call | solution.py:300
  41.0 0.6 %copy.8 = bf16[4,512]{1,0:T(4,128)(2,1)} copy(bf16[4,512]{1,0:T(4,128)(2,1)S(1)} %shard_map.64) | data formatting | bytes 8192
Async XLA Ops:
  0.0 1.0 %copy-start = (bf16[4,128,512]{2,1,0:T(8,128)(2,1)S(1)}, bf16[4,128,512]{2,1,0:T(8,128)(2,1)}, u32[]{:S(2)}) copy-start(bf16[4,128,512]{2,1,0:T(8,128)(2,1)} %w_uk_hbm.1) | copy-start | bytes 1572868
  1.0 1.0 %copy-start.1 = (bf16[4,512,128]{2,1,0:T(8,128)(2,1)S(1)}, bf16[4,512,128]{2,1,0:T(8,128)(2,1)}, u32[]{:S(2)}) copy-start(bf16[4,512,128]{2,1,0:T(8,128)(2,1)} %w_uv_hbm.1) | copy-start | bytes 1572868
  2.1 0.7 %copy-start.2 = (bf16[4,4,128]{2,1,0:T(4,128)(2,1)S(1)}, bf16[4,4,128]{2,1,0:T(4,128)(2,1)}, u32[]{:S(2)}) copy-start(bf16[4,4,128]{2,1,0:T(4,128)(2,1)} %q_nope.1) | copy-start | bytes 12292
  2.8 0.7 %copy-start.3 = (bf16[4,4,64]{2,1,0:T(4,128)(2,1)S(1)}, bf16[4,4,64]{2,1,0:T(4,128)(2,1)}, u32[]{:S(2)}) copy-start(bf16[4,4,64]{2,1,0:T(4,128)(2,1)} %q_rope.1) | copy-start | bytes 6148
  3.5 0.7 %copy-start.4 = (s32[4]{0:T(128)S(1)}, s32[4]{0:T(128)}, u32[]{:S(2)}) copy-start(s32[4]{0:T(128)} %lengths.1) | copy-start | bytes 52

commit v2 on v1

v2 whole, which is shorter than its diff:
```python
import functools
import math

import jax
import jax.numpy as jnp
from jax import lax
from jax.experimental import pallas as pl
from jax.experimental.pallas import tpu as pltpu
from jax.sharding import PartitionSpec as P

MESH = pl.DeviceIdType.MESH
F32 = jnp.float32
BF16 = jnp.bfloat16
NX, NZ = 4, 8
NB, NH = 4, 4
LANES = 128
DEAD = -1e30
CHUNK = 512


def to_lanes(column, rows):
    row = lax.broadcasted_iota(jnp.int32, (rows, LANES), 0)
    lane = lax.broadcasted_iota(jnp.int32, (rows, LANES), 1)
    return jnp.sum(jnp.where(row == lane, column, 0.0), axis=0, keepdims=True)


def to_column(row, picked):
    return jnp.sum(jnp.where(picked, row, 0.0), axis=1, keepdims=True)


def kernel(
    scale,
    lengths_hbm,
    q_nope_hbm,
    q_rope_hbm,
    w_uk_hbm,
    w_uv_hbm,
    cache_hbm,
    out,
    lengths,
    q_nope,
    q_rope,
    w_uk,
    w_uv,
    cache,
    gathered,
    ropes,
    flat,
    rope_flat,
    query,
    scores,
    probs,
    x_send,
    x_recv,
    x_stat,
    turn,
    z_send,
    z_recv,
    z_stat,
    latent,
    local_sem,
    send_sem,
    gz_sem,
    gx_sem,
    rx_sem,
    rz_sem,
    rxs_sem,
    rzs_sem,
):
    req = lax.axis_index("req")
    kv = lax.axis_index("kv")
    z = lax.div(kv, NX)
    x = lax.rem(kv, NX)
    split_len = cache.shape[2]
    latent_width = w_uk.shape[2]
    z_order = (4, 3, 5, 2, 6, 1, 7)
    x_order = (2, 1, 3)

    def z_at(d):
        return lax.rem(z + d, NZ)

    def x_at(d):
        return lax.rem(x + d, NX)

    barrier = pltpu.get_barrier_semaphore()
    for d in z_order:
        pl.semaphore_signal(barrier, inc=1, device_id=(req, z_at(d) * NX + x), device_id_type=MESH)
    for d in x_order:
        pl.semaphore_signal(barrier, inc=1, device_id=(req, z * NX + x_at(d)), device_id_type=MESH)

    first_copies = [
        pltpu.make_async_copy(q_rope_hbm, q_rope, local_sem.at[6]),
        pltpu.make_async_copy(q_nope_hbm, q_nope, local_sem.at[7]),
        pltpu.make_async_copy(w_uk_hbm, w_uk, local_sem.at[4]),
    ]
    for copy in first_copies:
        copy.start()
    lengths_copy = pltpu.make_async_copy(lengths_hbm, lengths, local_sem.at[8])
    lengths_copy.start()

    def cache_copy(b):
        return pltpu.make_async_copy(cache_hbm.at[b], cache.at[b], local_sem.at[b])

    for b in range(NB):
        cache_copy(b).start()
    uv_copy = pltpu.make_async_copy(w_uv_hbm, w_uv, local_sem.at[5])
    uv_copy.start()

    def to_z(src, dst, kind, sem, d):
        return pltpu.make_async_remote_copy(
            src_ref=src,
            dst_ref=dst,
            send_sem=send_sem.at[kind],
            recv_sem=sem,
            device_id=(req, z_at(d) * NX + x),
            device_id_type=MESH,
        )

    def to_x(src, dst, kind, sem, d):
        return pltpu.make_async_remote_copy(
            src_ref=src,
            dst_ref=dst,
            send_sem=send_sem.at[kind],
            recv_sem=sem,
            device_id=(req, z * NX + x_at(d)),
            device_id_type=MESH,
        )

    def take(ref, sem):
        pltpu.make_async_copy(ref, ref, sem).wait()

    for copy in first_copies:
        copy.wait()
    for b in range(NB):
        flat[b * NH : (b + 1) * NH, :] = q_nope[b].astype(F32)
        rope = q_rope[b].astype(F32)
        for h in range(NH):
            r = b * 2 + h // 2
            rope_flat[r : r + 1, (h % 2) * 64 : (h % 2) * 64 + 64] = rope[h : h + 1, :]
    ropes[x, z] = rope_flat[0:8, :].astype(BF16)
    rows = flat[0:16, :]
    head = lax.rem(lax.broadcasted_iota(jnp.int32, (16, LANES), 0), NH)
    q_lat = jnp.zeros((16, latent_width), F32)
    for h in range(NH):
        own = jnp.where(head == h, rows, 0.0).astype(BF16)
        q_lat = q_lat + jnp.dot(own, w_uk[h], preferred_element_type=F32)
    for b in range(NB):
        for j in range(4):
            flat[b * 16 + j * NH : b * 16 + (j + 1) * NH, :] = q_lat[
                b * NH : (b + 1) * NH, j * LANES : (j + 1) * LANES
            ]
    for b in range(NB):
        gathered[b, x, z] = flat[b * 16 : (b + 1) * 16, :].astype(BF16)

    pl.semaphore_wait(barrier, NZ - 1 + NX - 1)

    for d in z_order:
        to_z(ropes.at[x, z], ropes.at[x, z], 1, gz_sem.at[NB], d).start()
    for b in range(NB):
        for d in z_order:
            to_z(gathered.at[b, x, z], gathered.at[b, x, z], 0, gz_sem.at[b], d).start()
    take(ropes.at[0, pl.ds(0, NZ - 1)], gz_sem.at[NB])
    for d in x_order:
        to_x(ropes.at[x], ropes.at[x], 3, gx_sem.at[NB], d).start()
    for b in range(NB):
        take(gathered.at[b, 0, pl.ds(0, NZ - 1)], gz_sem.at[b])
        for d in x_order:
            to_x(gathered.at[b, x], gathered.at[b, x], 2, gx_sem.at[b], d).start()

    take(ropes.at[pl.ds(0, NX - 1)], gx_sem.at[NB])
    rope_flat[...] = ropes[...].reshape(NX * NZ * 8, LANES).astype(F32)

    lengths_copy.wait()
    position = kv * split_len + lax.broadcasted_iota(jnp.int32, (1, CHUNK), 1)

    def attend(b, carry):
        take(gathered.at[b, pl.ds(0, NX - 1)], gx_sem.at[b])
        flat[...] = gathered[b].reshape(NX * NZ * 16, LANES).astype(F32)
        for xs in range(NX):
            for hp in range(0, NH, 2):
                at = xs * 32 + hp * 8
                for j in range(4):
                    pair = [
                        flat[pl.ds(xs * 128 + j * NH + h, 8, stride=16), :] for h in (hp, hp + 1)
                    ]
                    query[at : at + 16, j * LANES : (j + 1) * LANES] = jnp.concatenate(
                        pair, axis=0
                    ).astype(BF16)
                both = rope_flat[pl.ds(xs * 64 + b * 2 + hp // 2, 8, stride=8), :]
                query[at : at + 16, 512:576] = jnp.concatenate(
                    [both[:, 0:64], both[:, 64:128]], axis=0
                ).astype(BF16)
        cache_copy(b).wait()
        q = query[...]
        length = lengths[b]
        peak = None
        for c in range(0, split_len, CHUNK):
            s = jnp.dot(q, cache[b, :, c : c + CHUNK], preferred_element_type=F32)
            s = jnp.where(position + c < length, s, DEAD)
            scores[:, c : c + CHUNK] = s
            for k in range(0, CHUNK, LANES):
                piece = s[:, k : k + LANES]
                peak = piece if peak is None else jnp.maximum(peak, piece)
        top = jnp.max(peak, axis=1, keepdims=True) * scale
        total = jnp.zeros((128, LANES), F32)
        for c in range(0, split_len, CHUNK):
            p = jnp.exp2(scores[:, c : c + CHUNK] * scale - top)
            probs[:, c : c + CHUNK] = p.astype(BF16)
            for k in range(0, CHUNK, LANES):
                total = total + p[:, k : k + LANES]
        o = lax.dot_general(
            probs[...], cache[b, 0:512, :], (((1,), (1,)), ((), ())), preferred_element_type=F32
        )
        x_send[b] = o.astype(BF16)
        x_stat[b, x, 0:1, :] = to_lanes(top, 128)
        x_stat[b, x, 1:2, :] = to_lanes(jnp.sum(total, axis=1, keepdims=True), 128)
        for d in x_order:
            to_x(x_stat.at[b, x], x_stat.at[b, x], 5, rxs_sem.at[b], d).start()
            rows_there = pl.ds(pl.multiple_of(x_at(d) * 32, 32), 32)
            to_x(x_send.at[b, rows_there], x_recv.at[b, x], 4, rx_sem.at[b], d).start()
        return carry

    lax.fori_loop(0, NB, attend, 0)

    def reduce_x(b, carry):
        take(x_stat.at[b, pl.ds(0, NX - 1)], rxs_sem.at[b])
        take(x_recv.at[b, pl.ds(0, NX - 1)], rx_sem.at[b])
        row = lax.broadcasted_iota(jnp.int32, (32, LANES), 0)
        lane = lax.broadcasted_iota(jnp.int32, (32, LANES), 1)
        picked = lane == row + x * 32
        tops, sums = [], []
        for d in (0,) + x_order:
            stat = x_stat[b, x_at(d)]
            tops.append(to_column(stat[0:1, :], picked))
            sums.append(to_column(stat[1:2, :], picked))
        top = functools.reduce(jnp.maximum, tops)
        weights = [jnp.exp2(t - top) for t in tops]
        total = sum(w * s for w, s in zip(weights, sums))
        z_stat[b, z, 0:1, :] = to_lanes(top, 32)
        z_stat[b, z, 1:2, :] = to_lanes(total, 32)
        acc = x_send[b, pl.ds(pl.multiple_of(x * 32, 32), 32), :].astype(F32) * weights[0]
        for d, w in zip(x_order, weights[1:]):
            acc = acc + x_recv[b, x_at(d)].astype(F32) * w
        for h in range(NH):
            for j in range(4):
                r = h * 4 + j
                turn[r * 8 : r * 8 + 8, :] = acc[h * 8 : h * 8 + 8, j * LANES : (j + 1) * LANES]
        for zs in range(NZ):
            z_send[b, zs] = turn[pl.ds(zs, 16, stride=8), :].astype(BF16)
        for d in z_order:
            to_z(z_stat.at[b, z], z_stat.at[b, z], 7, rzs_sem.at[b], d).start()
            to_z(z_send.at[b, z_at(d)], z_recv.at[b, z], 6, rz_sem.at[b], d).start()
        return carry

    lax.fori_loop(0, NB, reduce_x, 0)

    def reduce_z(b, carry):
        take(z_stat.at[b, pl.ds(0, NZ - 1)], rzs_sem.at[b])
        take(z_recv.at[b, pl.ds(0, NZ - 1)], rz_sem.at[b])
        row = lax.broadcasted_iota(jnp.int32, (16, LANES), 0)
        lane = lax.broadcasted_iota(jnp.int32, (16, LANES), 1)
        picked = lane == lax.div(row, 4) * 8 + z
        tops, sums = [], []
        for d in (0,) + z_order:
            stat = z_stat[b, z_at(d)]
            tops.append(to_column(stat[0:1, :], picked))
            sums.append(to_column(stat[1:2, :], picked))
        top = functools.reduce(jnp.maximum, tops)
        weights = [jnp.exp2(t - top) for t in tops]
        total = sum(w * s for w, s in zip(weights, sums))
        acc = z_send[b, z].astype(F32) * weights[0]
        for d, w in zip(z_order, weights[1:]):
            acc = acc + z_recv[b, z_at(d)].astype(F32) * w
        latent[pl.ds(pl.multiple_of(b * 16, 16), 16), :] = acc / total
        return carry

    lax.fori_loop(0, NB, reduce_z, 0)

    uv_copy.wait()
    for h in range(NH):
        lat = jnp.concatenate(
            [latent[pl.ds(h * 4 + j, NB, stride=16), :] for j in range(4)], axis=1
        ).astype(BF16)
        out[:, h * LANES : (h + 1) * LANES] = jnp.dot(
            lat, w_uv[h], preferred_element_type=F32
        ).astype(BF16)

    take(gathered.at[pl.ds(0, NB), 0, pl.ds(0, NZ - 1)], send_sem.at[0])
    take(ropes.at[0, pl.ds(0, NZ - 1)], send_sem.at[1])
    take(gathered.at[pl.ds(0, NB), pl.ds(0, NX - 1)], send_sem.at[2])
    take(ropes.at[pl.ds(0, NX - 1)], send_sem.at[3])
    take(x_recv.at[pl.ds(0, NB), pl.ds(0, NX - 1)], send_sem.at[4])
    take(x_stat.at[pl.ds(0, NB), pl.ds(0, NX - 1)], send_sem.at[5])
    take(z_recv.at[pl.ds(0, NB), pl.ds(0, NZ - 1)], send_sem.at[6])
    take(z_stat.at[pl.ds(0, NB), pl.ds(0, NZ - 1)], send_sem.at[7])


def local(q_nope, q_rope, cache, lengths, w_uk, w_uv):
    scale = (q_nope.shape[2] + q_rope.shape[2]) ** (-0.5) * math.log2(math.e)
    cache_t = jnp.swapaxes(cache, 1, 2)
    vmem = pl.BlockSpec(memory_space=pltpu.VMEM)
    hbm = pl.BlockSpec(memory_space=pl.ANY)
    dma = pltpu.SemaphoreType.DMA
    return pl.pallas_call(
        functools.partial(kernel, scale),
        out_shape=jax.ShapeDtypeStruct((NB, NH * w_uv.shape[2]), BF16),
        in_specs=[hbm] * 6,
        out_specs=vmem,
        scratch_shapes=[
            pltpu.SMEM(lengths.shape, jnp.int32),
            pltpu.VMEM(q_nope.shape, BF16),
            pltpu.VMEM(q_rope.shape, BF16),
            pltpu.VMEM(w_uk.shape, BF16),
            pltpu.VMEM(w_uv.shape, BF16),
            pltpu.VMEM(cache_t.shape, BF16),
            pltpu.VMEM((NB, NX, NZ, 16, LANES), BF16),
            pltpu.VMEM((NX, NZ, 8, LANES), BF16),
            pltpu.VMEM((NX * NZ * 16, LANES), F32),
            pltpu.VMEM((NX * NZ * 8, LANES), F32),
            pltpu.VMEM((128, 576), BF16),
            pltpu.VMEM((128, cache_t.shape[2]), F32),
            pltpu.VMEM((128, cache_t.shape[2]), BF16),
            pltpu.VMEM((NB, 128, 512), BF16),
            pltpu.VMEM((NB, NX, 32, 512), BF16),
            pltpu.VMEM((NB, NX, 2, LANES), F32),
            pltpu.VMEM((128, LANES), F32),
            pltpu.VMEM((NB, NZ, 16, LANES), BF16),
            pltpu.VMEM((NB, NZ, 16, LANES), BF16),
            pltpu.VMEM((NB, NZ, 2, LANES), F32),
            pltpu.VMEM((NB * 16, LANES), F32),
            dma((9,)),
            dma((8,)),
            dma((NB + 1,)),
            dma((NB + 1,)),
            dma((NB,)),
            dma((NB,)),
            dma((NB,)),
            dma((NB,)),
        ],
        compiler_params=pltpu.CompilerParams(
            collective_id=0, has_side_effects=True, vmem_limit_bytes=48 * 2**20
        ),
    )(*[pltpu.with_memory_space_constraint(a, pltpu.HBM) for a in (lengths, q_nope, q_rope, w_uk, w_uv, cache_t)])


def solution(mesh):
    in_specs = (
        P("req", "kv", None),
        P("req", "kv", None),
        P("req", "kv", None),
        P("req"),
        P("kv", None, None),
        P("kv", None, None),
    )
    return jax.shard_map(
        local, mesh=mesh, in_specs=in_specs, out_specs=P("req", "kv"), check_vma=False
    )
```

time: 41.8 us -> 34.2 us (0.82)
  local copies, waits for them, and re-layouts: 4.7 us -> 0.6 us
  Pallas kernels: 36.9 us -> 33.5 us
    unnamed x11 -> x1, local copies, waits for them, and re-layouts: 4.7 us -> 0.6 us
    pallas_call x1, Pallas kernels: 36.9 us -> 33.5 us  [local(): pl.pallas_call(functools.partial(kernel, scale), out_shape=jax.ShapeDtype...]
where the time goes in v2:
time: 34.2 us; the launch traced here: 34.1 us
  Pallas kernels  33.5 us (98%)
  local copies, waits for them, and re-layouts  0.6 us (2%)
    pallas_call x1, Pallas kernels, local(): pl.pallas_call(functools.partial(kernel, scale), out_shape=jax.ShapeDtype...  33.5 us

profile of v2, /device:TPU:8, one launch (start us, length us, event | category | flops | bytes accessed | tf_op | source)
XLA Modules:
  0.0 34.1 jit_solution(5923121157530410667)
XLA Ops:
  0.0 33.5 %shard_map.64 = bf16[4,512]{1,0:T(4,128)(2,1)S(1)} custom-call(s32[4]{0:T(128)} %lengths_hbm.1, bf16[4,4,128]{2,1,0:T(4,128)(2,1)} %q_nope_hbm.1, bf16[4,4,64]{2,1,0:T(4,128)(2,1)} %q_rope_hbm.1, bf16[4,128,512]{2,1,0:T(8,128)(2,1)} %w_uk_hbm.1, bf16[4,512,128]{2,1,0:T(8,128)(2,1)} %w_uv_hbm.1, bf16[4,576,2048]{2,1,0:T(8,128)(2,1)} %bitcast.1), custom_call_target="tpu_custom_call" | custom-call | tf_op jit(solution)/shard_map/pallas_call | solution.py:304
  33.5 0.6 %copy.8 = bf16[4,512]{1,0:T(4,128)(2,1)} copy(bf16[4,512]{1,0:T(4,128)(2,1)S(1)} %shard_map.64) | data formatting | bytes 8192

commit v3 on v2

--- a/solution.py
+++ b/solution.py
@@ -43,6 +43,7 @@
     w_uk,
     w_uv,
     cache,
+    natural,
     gathered,
     ropes,
     flat,
@@ -159,13 +160,30 @@
     for b in range(NB):
         for d in z_order:
             to_z(gathered.at[b, x, z], gathered.at[b, x, z], 0, gz_sem.at[b], d).start()
+    def turn_cache(b, carry):
+        cache_copy(b).wait()
+        for c in range(0, split_len, 256):
+            natural[b, c : c + 256, :] = jnp.transpose(cache[b, 0:512, c : c + 256])
+        return carry
+
+    lax.fori_loop(0, NB, turn_cache, 0)
+
     take(ropes.at[0, pl.ds(0, NZ - 1)], gz_sem.at[NB])
     for d in x_order:
         to_x(ropes.at[x], ropes.at[x], 3, gx_sem.at[NB], d).start()
-    for b in range(NB):
+    def pass_on(b):
         take(gathered.at[b, 0, pl.ds(0, NZ - 1)], gz_sem.at[b])
         for d in x_order:
             to_x(gathered.at[b, x], gathered.at[b, x], 2, gx_sem.at[b], d).start()
+
+    core = lax.rem(req, 2)
+    for b in range(3):
+        pass_on(b)
+
+    @pl.when(core == 0)
+    def _():
+        for b in range(3, NB):
+            pass_on(b)
 
     take(ropes.at[pl.ds(0, NX - 1)], gx_sem.at[NB])
     rope_flat[...] = ropes[...].reshape(NX * NZ * 8, LANES).astype(F32)
@@ -190,7 +208,6 @@
                 query[at : at + 16, 512:576] = jnp.concatenate(
                     [both[:, 0:64], both[:, 64:128]], axis=0
                 ).astype(BF16)
-        cache_copy(b).wait()
         q = query[...]
         length = lengths[b]
         peak = None
@@ -208,9 +225,7 @@
             probs[:, c : c + CHUNK] = p.astype(BF16)
             for k in range(0, CHUNK, LANES):
                 total = total + p[:, k : k + LANES]
-        o = lax.dot_general(
-            probs[...], cache[b, 0:512, :], (((1,), (1,)), ((), ())), preferred_element_type=F32
-        )
+        o = jnp.dot(probs[...], natural[b], preferred_element_type=F32)
         x_send[b] = o.astype(BF16)
         x_stat[b, x, 0:1, :] = to_lanes(top, 128)
         x_stat[b, x, 1:2, :] = to_lanes(jnp.sum(total, axis=1, keepdims=True), 128)
@@ -218,6 +233,11 @@
             to_x(x_stat.at[b, x], x_stat.at[b, x], 5, rxs_sem.at[b], d).start()
             rows_there = pl.ds(pl.multiple_of(x_at(d) * 32, 32), 32)
             to_x(x_send.at[b, rows_there], x_recv.at[b, x], 4, rx_sem.at[b], d).start()
+
+        @pl.when((core == 1) & (b + 3 < NB))
+        def _():
+            pass_on(b + 3)
+
         return carry
 
     lax.fori_loop(0, NB, attend, 0)
@@ -313,6 +333,7 @@
             pltpu.VMEM(w_uk.shape, BF16),
             pltpu.VMEM(w_uv.shape, BF16),
             pltpu.VMEM(cache_t.shape, BF16),
+            pltpu.VMEM((NB, cache_t.shape[2], 512), BF16),
             pltpu.VMEM((NB, NX, NZ, 16, LANES), BF16),
             pltpu.VMEM((NX, NZ, 8, LANES), BF16),
             pltpu.VMEM((NX * NZ * 16, LANES), F32),

time: 34.2 us -> 32.5 us (0.950)
  Pallas kernels: 33.5 us -> 31.8 us
    pallas_call x1, Pallas kernels: 33.5 us -> 31.8 us  [local(): pl.pallas_call(functools.partial(kernel, scale), out_shape=jax.ShapeDtype...]
where the time goes in v3:
time: 32.5 us; the launch traced here: 32.4 us
  Pallas kernels  31.8 us (98%)
  local copies, waits for them, and re-layouts  0.6 us (2%)
    pallas_call x1, Pallas kernels, local(): pl.pallas_call(functools.partial(kernel, scale), out_shape=jax.ShapeDtype...  31.8 us

profile of v3, /device:TPU:8, one launch (start us, length us, event | category | flops | bytes accessed | tf_op | source)
XLA Modules:
  0.0 32.4 jit_solution(17547998141335404966)
XLA Ops:
  0.0 31.8 %shard_map.64 = bf16[4,512]{1,0:T(4,128)(2,1)S(1)} custom-call(s32[4]{0:T(128)} %lengths_hbm.1, bf16[4,4,128]{2,1,0:T(4,128)(2,1)} %q_nope_hbm.1, bf16[4,4,64]{2,1,0:T(4,128)(2,1)} %q_rope_hbm.1, bf16[4,128,512]{2,1,0:T(8,128)(2,1)} %w_uk_hbm.1, bf16[4,512,128]{2,1,0:T(8,128)(2,1)} %w_uv_hbm.1, bf16[4,576,2048]{2,1,0:T(8,128)(2,1)} %bitcast.1), custom_call_target="tpu_custom_call" | custom-call | tf_op jit(solution)/shard_map/pallas_call | solution.py:324
  31.8 0.6 %copy.8 = bf16[4,512]{1,0:T(4,128)(2,1)} copy(bf16[4,512]{1,0:T(4,128)(2,1)S(1)} %shard_map.64) | data formatting | bytes 8192

commit v4 on v3

--- a/solution.py
+++ b/solution.py
@@ -138,7 +138,7 @@
         for h in range(NH):
             r = b * 2 + h // 2
             rope_flat[r : r + 1, (h % 2) * 64 : (h % 2) * 64 + 64] = rope[h : h + 1, :]
-    ropes[x, z] = rope_flat[0:8, :].astype(BF16)
+    ropes[z, x] = rope_flat[0:8, :].astype(BF16)
     rows = flat[0:16, :]
     head = lax.rem(lax.broadcasted_iota(jnp.int32, (16, LANES), 0), NH)
     q_lat = jnp.zeros((16, latent_width), F32)
@@ -155,8 +155,8 @@
 
     pl.semaphore_wait(barrier, NZ - 1 + NX - 1)
 
-    for d in z_order:
-        to_z(ropes.at[x, z], ropes.at[x, z], 1, gz_sem.at[NB], d).start()
+    for d in x_order:
+        to_x(ropes.at[z, x], ropes.at[z, x], 3, gx_sem.at[NB], d).start()
     for b in range(NB):
         for d in z_order:
             to_z(gathered.at[b, x, z], gathered.at[b, x, z], 0, gz_sem.at[b], d).start()
@@ -166,11 +166,12 @@
             natural[b, c : c + 256, :] = jnp.transpose(cache[b, 0:512, c : c + 256])
         return carry
 
-    lax.fori_loop(0, NB, turn_cache, 0)
-
-    take(ropes.at[0, pl.ds(0, NZ - 1)], gz_sem.at[NB])
-    for d in x_order:
-        to_x(ropes.at[x], ropes.at[x], 3, gx_sem.at[NB], d).start()
+    lax.fori_loop(0, NB - 1, turn_cache, 0)
+
+    take(ropes.at[0, pl.ds(0, NX - 1)], gx_sem.at[NB])
+    for d in z_order:
+        to_z(ropes.at[z], ropes.at[z], 1, gz_sem.at[NB], d).start()
+    turn_cache(NB - 1, 0)
     def pass_on(b):
         take(gathered.at[b, 0, pl.ds(0, NZ - 1)], gz_sem.at[b])
         for d in x_order:
@@ -185,7 +186,7 @@
         for b in range(3, NB):
             pass_on(b)
 
-    take(ropes.at[pl.ds(0, NX - 1)], gx_sem.at[NB])
+    take(ropes.at[pl.ds(0, NZ - 1)], gz_sem.at[NB])
     rope_flat[...] = ropes[...].reshape(NX * NZ * 8, LANES).astype(F32)
 
     lengths_copy.wait()
@@ -204,7 +205,7 @@
                     query[at : at + 16, j * LANES : (j + 1) * LANES] = jnp.concatenate(
                         pair, axis=0
                     ).astype(BF16)
-                both = rope_flat[pl.ds(xs * 64 + b * 2 + hp // 2, 8, stride=8), :]
+                both = rope_flat[pl.ds(xs * 8 + b * 2 + hp // 2, 8, stride=32), :]
                 query[at : at + 16, 512:576] = jnp.concatenate(
                     [both[:, 0:64], both[:, 64:128]], axis=0
                 ).astype(BF16)
@@ -306,9 +307,9 @@
         ).astype(BF16)
 
     take(gathered.at[pl.ds(0, NB), 0, pl.ds(0, NZ - 1)], send_sem.at[0])
-    take(ropes.at[0, pl.ds(0, NZ - 1)], send_sem.at[1])
+    take(ropes.at[pl.ds(0, NZ - 1)], send_sem.at[1])
     take(gathered.at[pl.ds(0, NB), pl.ds(0, NX - 1)], send_sem.at[2])
-    take(ropes.at[pl.ds(0, NX - 1)], send_sem.at[3])
+    take(ropes.at[0, pl.ds(0, NX - 1)], send_sem.at[3])
     take(x_recv.at[pl.ds(0, NB), pl.ds(0, NX - 1)], send_sem.at[4])
     take(x_stat.at[pl.ds(0, NB), pl.ds(0, NX - 1)], send_sem.at[5])
     take(z_recv.at[pl.ds(0, NB), pl.ds(0, NZ - 1)], send_sem.at[6])
@@ -335,7 +336,7 @@
             pltpu.VMEM(cache_t.shape, BF16),
             pltpu.VMEM((NB, cache_t.shape[2], 512), BF16),
             pltpu.VMEM((NB, NX, NZ, 16, LANES), BF16),
-            pltpu.VMEM((NX, NZ, 8, LANES), BF16),
+            pltpu.VMEM((NZ, NX, 8, LANES), BF16),
             pltpu.VMEM((NX * NZ * 16, LANES), F32),
             pltpu.VMEM((NX * NZ * 8, LANES), F32),
             pltpu.VMEM((128, 576), BF16),

time: 32.5 us -> 31.9 us (0.982)
  Pallas kernels: 31.8 us -> 31.2 us
    pallas_call x1, Pallas kernels: 31.8 us -> 31.2 us  [local(): pl.pallas_call(functools.partial(kernel, scale), out_shape=jax.ShapeDtype...]
where the time goes in v4:
time: 31.9 us; the launch traced here: 31.8 us
  Pallas kernels  31.2 us (98%)
  local copies, waits for them, and re-layouts  0.6 us (2%)
    pallas_call x1, Pallas kernels, local(): pl.pallas_call(functools.partial(kernel, scale), out_shape=jax.ShapeDtype...  31.2 us

profile of v4, /device:TPU:8, one launch (start us, length us, event | category | flops | bytes accessed | tf_op | source)
XLA Modules:
  0.0 31.8 jit_solution(7345840615040389469)
XLA Ops:
  0.0 31.2 %shard_map.64 = bf16[4,512]{1,0:T(4,128)(2,1)S(1)} custom-call(s32[4]{0:T(128)} %lengths_hbm.1, bf16[4,4,128]{2,1,0:T(4,128)(2,1)} %q_nope_hbm.1, bf16[4,4,64]{2,1,0:T(4,128)(2,1)} %q_rope_hbm.1, bf16[4,128,512]{2,1,0:T(8,128)(2,1)} %w_uk_hbm.1, bf16[4,512,128]{2,1,0:T(8,128)(2,1)} %w_uv_hbm.1, bf16[4,576,2048]{2,1,0:T(8,128)(2,1)} %bitcast.1), custom_call_target="tpu_custom_call" | custom-call | tf_op jit(solution)/shard_map/pallas_call | solution.py:325
  31.2 0.6 %copy.8 = bf16[4,512]{1,0:T(4,128)(2,1)} copy(bf16[4,512]{1,0:T(4,128)(2,1)S(1)} %shard_map.64) | data formatting | bytes 8192

commit v5 on v4

--- a/solution.py
+++ b/solution.py
@@ -295,7 +295,7 @@
         latent[pl.ds(pl.multiple_of(b * 16, 16), 16), :] = acc / total
         return carry
 
-    lax.fori_loop(0, NB, reduce_z, 0)
+    lax.fori_loop(0, NB, reduce_z, 0, unroll=True)
 
     uv_copy.wait()
     for h in range(NH):

time: 31.9 us -> 31.9 us (level)
  no operation moved by 1% of the time
where the time goes in v5:
time: 31.9 us; the launch traced here: 31.8 us
  Pallas kernels  31.2 us (98%)
  local copies, waits for them, and re-layouts  0.6 us (2%)
    pallas_call x1, Pallas kernels, local(): pl.pallas_call(functools.partial(kernel, scale), out_shape=jax.ShapeDtype...  31.2 us

profile of v5, /device:TPU:8, one launch (start us, length us, event | category | flops | bytes accessed | tf_op | source)
XLA Modules:
  0.0 31.8 jit_solution(6665473325154658042)
XLA Ops:
  0.0 31.2 %shard_map.64 = bf16[4,512]{1,0:T(4,128)(2,1)S(1)} custom-call(s32[4]{0:T(128)} %lengths_hbm.1, bf16[4,4,128]{2,1,0:T(4,128)(2,1)} %q_nope_hbm.1, bf16[4,4,64]{2,1,0:T(4,128)(2,1)} %q_rope_hbm.1, bf16[4,128,512]{2,1,0:T(8,128)(2,1)} %w_uk_hbm.1, bf16[4,512,128]{2,1,0:T(8,128)(2,1)} %w_uv_hbm.1, bf16[4,576,2048]{2,1,0:T(8,128)(2,1)} %bitcast.1), custom_call_target="tpu_custom_call" | custom-call | tf_op jit(solution)/shard_map/pallas_call | solution.py:325
  31.2 0.6 %copy.8 = bf16[4,512]{1,0:T(4,128)(2,1)} copy(bf16[4,512]{1,0:T(4,128)(2,1)S(1)} %shard_map.64) | data formatting | bytes 8192
